TPU v7x, 32 devices: a whole 2x2x4 slice. The times are simulated.
32 devices in a mesh: replica: 2 (over y), section: 4 (over x, core), tensor: 4 (over z).
Axes of the slice: x: 2, y: 2, z: 4, core: 2. Of those that a mesh axis runs over, the one named last changes fastest.
Arguments:
- hidden_in: bfloat16 [256, 8192], P('replica', 'tensor'), may hold values from -6 to 6
- lengths: int32 [2], P('replica'), may hold values from 1 to 128, 160 in all
- norm_gain: float32 [4, 8192], P('section'), may hold values from 0.1 to 1.9
- q_tiles: bfloat16 [4, 8192, 4096], P('section', 'replica', 'tensor'), may hold values from -4 to 4
- q_scales: bfloat16 [4, 64, 32], P('section', 'replica', 'tensor'), as said below
- kv_tiles: bfloat16 [4, 8192, 2048], P('section', 'replica', 'tensor'), may hold values from -4 to 4
- kv_scales: bfloat16 [4, 64, 16], P('section', 'replica', 'tensor'), as said below
- out_weight: bfloat16 [4, 4096, 8192], P('section', 'tensor'), may hold values from -0.09375 to 0.09375
Outputs:
- layer_outputs: bfloat16 [4, 256, 8192], P('section', 'replica', 'tensor')
- key_values: bfloat16 [4, 256, 2048], P('section', 'replica', 'tensor')
Inputs may be any that keep to these rules, and one draw needn't show every extreme that they name: `q_scales`: every tile scale is positive. `kv_scales`: every tile scale is positive.
All inputs are finite; a program needn't handle non-finite values. No bound on the sum of `lengths` on one device may be relied on, other than what follows from the above.
Results may differ from a plain program's by a relative error of at most 0.015.
Values may be sent and summed in bfloat16 or wider, within the bound.
No kernel may reach another device: no remote copies, remote signals or barrier semaphores. Data moves between devices by JAX's collectives and lax.ppermute only.
A program may use at most 192 MiB of HBM per device.

v0:
```python
import jax
import jax.numpy as jnp
from jax import lax
from jax.sharding import PartitionSpec as P

HEAD = 128
BLOCK = 128
SPAN = 32


rope_base = 1000000.0
norm_eps = 1e-06


def from_behind(value, axis, steps):
    count = lax.axis_size(axis)
    first, last = (max(0, -steps), min(count, count - steps))
    return lax.ppermute(value, axis, [(source, source + steps) for source in range(first, last)])


def dequantize(tiles, scales, block):
    rows, cols = tiles.shape
    grid = tiles.reshape(rows // block, block, cols // block, block).astype(jnp.float32)
    scaled = grid * scales.astype(jnp.float32)[:, None, :, None]
    return scaled.reshape(rows, cols).astype(jnp.bfloat16)


def rotate(values, positions):
    half = values.shape[-1] // 2
    freq = rope_base ** (-jnp.arange(half, dtype=jnp.float32) / half)
    angle = positions.astype(jnp.float32)[:, None] * freq[None, :]
    cosine = jnp.cos(angle)[:, None, :]
    sine = jnp.sin(angle)[:, None, :]
    first = values[..., :half]
    second = values[..., half:]
    return jnp.concatenate([first * cosine - second * sine, second * cosine + first * sine], -1)


def per_device(hidden_in, lengths, norm_gain, q_tiles, q_scales, kv_tiles, kv_scales, out_weight):
    section = lax.axis_index("section")
    sections = lax.axis_size("section")
    rows, width = hidden_in.shape
    blocks = rows // SPAN
    q_all, qs_all, kv_all, kvs_all = (
        lax.all_gather(q_tiles, "replica", axis=1, tiled=True),
        lax.all_gather(q_scales, "replica", axis=1, tiled=True),
        lax.all_gather(kv_tiles, "replica", axis=1, tiled=True),
        lax.all_gather(kv_scales, "replica", axis=1, tiled=True),
    )
    w_query = dequantize(q_all[0], qs_all[0], BLOCK)
    w_keyval = dequantize(kv_all[0], kvs_all[0], BLOCK)
    q_cols = w_query.shape[1]
    kv_cols = w_keyval.shape[1]
    kv_heads = kv_cols // (2 * HEAD)
    q_heads = q_cols // HEAD
    group = q_heads // kv_heads
    length = lengths[0]
    gain = norm_gain[0]
    w_out = out_weight[0]
    key_index = jnp.arange(rows, dtype=jnp.int32)

    def layer_block(full, cache, start):
        values = full.astype(jnp.float32)
        scale = lax.rsqrt(jnp.mean(values * values, -1, keepdims=True) + norm_eps)
        normed = (values * scale * gain).astype(jnp.bfloat16)
        positions = start + jnp.arange(SPAN, dtype=jnp.int32)
        query = jnp.dot(normed, w_query, preferred_element_type=jnp.float32).reshape(
            SPAN, q_heads, HEAD
        )
        query = rotate(query, positions).astype(jnp.bfloat16).reshape(SPAN, kv_heads, group, HEAD)
        keyval = jnp.dot(normed, w_keyval, preferred_element_type=jnp.float32).reshape(
            SPAN, kv_heads, 2, HEAD
        )
        keys = rotate(keyval[:, :, 0], positions).astype(jnp.bfloat16)
        vals = keyval[:, :, 1].astype(jnp.bfloat16)
        fresh = jnp.stack([keys, vals], 2).reshape(SPAN, kv_cols)
        cache = lax.dynamic_update_slice_in_dim(cache, fresh, start, 0)
        cached = cache.reshape(rows, kv_heads, 2, HEAD)
        scores = jnp.einsum(
            "ikgd,jkd->kgij", query, cached[:, :, 0], preferred_element_type=jnp.float32
        )
        scores = scores / jnp.sqrt(jnp.float32(HEAD))
        mask = (key_index[None, :] <= positions[:, None]) & (key_index[None, :] < length)
        mask = mask[None, None, :, :]
        scores = jnp.where(mask, scores, -jnp.inf)
        top = jnp.max(scores, -1, keepdims=True)
        expo = jnp.where(mask, jnp.exp(scores - top), 0.0)
        probs = (expo / jnp.sum(expo, -1, keepdims=True)).astype(jnp.bfloat16)
        attended = jnp.einsum(
            "kgij,jkd->ikgd", probs, cached[:, :, 1], preferred_element_type=jnp.float32
        )
        attended = attended.astype(jnp.bfloat16).reshape(SPAN, q_cols)
        partial_value = jnp.dot(attended, w_out, preferred_element_type=jnp.float32)
        rounded = lax.optimization_barrier(partial_value.astype(jnp.bfloat16))
        return (rounded.astype(jnp.float32), cache)

    def resting(full, cache, start):
        return (jnp.zeros((SPAN, w_out.shape[1]), jnp.float32), cache)

    cache_init = jnp.zeros((rows, kv_cols), jnp.bfloat16)
    result_init = jnp.zeros((rows, width), jnp.bfloat16)
    ticks = blocks + sections - 1

    def tick(step, state):
        inbox, cache, layer_out = state
        block = step - section
        active = (block >= 0) & (block < blocks)
        start = jnp.clip(block, 0, blocks - 1) * SPAN
        entering = lax.dynamic_slice_in_dim(hidden_in, start, SPAN, 0)
        current = jnp.where(section == 0, entering, inbox)
        full = lax.all_gather(current, "tensor", axis=1, tiled=True)
        partial_value, cache = lax.cond(active, layer_block, resting, full, cache, start)
        summed = lax.psum_scatter(partial_value, "tensor", scatter_dimension=1, tiled=True)
        result = (current.astype(jnp.float32) + summed).astype(jnp.bfloat16)
        kept = lax.dynamic_slice_in_dim(layer_out, start, SPAN, 0)
        layer_out = lax.dynamic_update_slice_in_dim(
            layer_out, jnp.where(active, result, kept), start, 0
        )
        inbox = from_behind(result, "section", 1)
        return (inbox, cache, layer_out)

    inbox_init = jnp.zeros((SPAN, width), jnp.bfloat16)
    final = lax.fori_loop(0, ticks, tick, (inbox_init, cache_init, result_init))
    return (final[2][None], final[1][None])


def solution(mesh):
    in_specs = (
        P("replica", "tensor"),
        P("replica"),
        P("section", None),
        P("section", "replica", "tensor"),
        P("section", "replica", "tensor"),
        P("section", "replica", "tensor"),
        P("section", "replica", "tensor"),
        P("section", "tensor", None),
    )
    out_specs = (P("section", "replica", "tensor"), P("section", "replica", "tensor"))
    return jax.shard_map(
        per_device, mesh=mesh, in_specs=in_specs, out_specs=out_specs, check_vma=False
    )
```

profile of v0, /device:TPU:3, one launch (start us, length us, event | category | flops | bytes accessed | tf_op | source)
XLA Modules:
  0.0 874.8 jit_solution(880077015238309617)
XLA Ops:
  9.4 3.3 all_gather.23
  13.5 3.3 all_gather.21
  16.8 98.0 %all-gather.3.cloned.1.call-done = bf16[1,8192,512]{2,1,0:T(8,128)(2,1)} async-done(((bf16[1,4096,512]{2,1,0:T(8,128)(2,1)}), bf16[1,8192,512]{2,1,0:T(8,128)(2,1)}) %all-gather.3.cloned.1.call-update) | async-done | bytes 8388624 | tf_op jit(solution)/shard_map/all_gather | solution.py:47
  114.8 2.8 mul.134
  118.3 6.7 fusion.32
  124.9 190.3 %all-gather.5.cloned.1.call-done = bf16[1,8192,1024]{2,1,0:T(8,128)(2,1)} async-done(((bf16[1,4096,1024]{2,1,0:T(8,128)(2,1)}), bf16[1,8192,1024]{2,1,0:T(8,128)(2,1)}) %all-gather.5.cloned.1.call-update) | async-done | bytes 16777232 | tf_op jit(solution)/shard_map/all_gather | solution.py:45
  315.3 2.8 mul.137
  318.0 18.0 %fusion.31 = bf16[8192,1024]{1,0:T(8,128)(2,1)} fusion(f32[1024,8,8,128]{3,2,1,0:T(8,128)S(1)} %bitcast.73, bf16[1,8192,1024]{2,1,0:T(8,128)(2,1)} %all-gather.5.cloned.1.call-done), kind=kLoop, calls=%fused_computation.52 | loop fusion | flops 25165824 | bytes 67108864 | tf_op jit(solution)/shard_map/convert_element_type | solution.py:25
  336.1 531.4 %while.23 = (s32[]{:T(128)}, bf16[32,2048]{1,0:T(8,128)(2,1)S(1)}, bf16[128,512]{0,1:T(8,128)(2,1)S(1)}, bf16[128,2048]{1,0:T(8,128)(2,1)S(1)}, pred[]{:T(512)},...) while((s32[]{:T(128)}, bf16[32,2048]{1,0:T(8,128)(2,1)S(1)}, ...), condition=%wide.region_7.8_spmd.clone.clone, body=%wide.region_0.7_spmd.clone.clone.sunk | while | flops 1372007296 | bytes 58848148 | solution.py:123
  337.1 14.2 %all_gather.27 = bf16[32,8192]{1,0:T(8,128)(2,1)S(1)} all-gather(bf16[32,2048]{1,0:T(8,128)(2,1)S(1)} %dynamic-slice_select_fusion.2), channel_id=1, replica_groups=mesh['replica'=2,'section'=4,'tensor'=4] {'tensor'}, dimensions={1}, use_global_device_ids=true | all-gather | bytes 655360 | tf_op jit(solution)/shard_map/while/body/eval_jaxpr/all_gather | solution.py:111
  351.4 1.0 copy-done
  352.4 54.5 %reduce-scatter.2.cloned.1.call-done = f32[32,2048]{1,0:T(8,128)} async-done(((f32[32,8192]{1,0:T(8,128)}), f32[32,2048]{1,0:T(8,128)}) %reduce-scatter.2.cloned.1.call-update) | async-done | bytes 262160 | tf_op jit(solution)/shard_map/while/body/eval_jaxpr/reduce_scatter | solution.py:113
  406.9 1.0 select_dynamic-update-slice_fusion.2
  407.9 1.3 collective-permute-start
  409.2 2.3 collective-permute-done
  412.4 13.5 %all_gather.27 = bf16[32,8192]{1,0:T(8,128)(2,1)S(1)} all-gather(bf16[32,2048]{1,0:T(8,128)(2,1)S(1)} %dynamic-slice_select_fusion.2), channel_id=1, replica_groups=mesh['replica'=2,'section'=4,'tensor'=4] {'tensor'}, dimensions={1}, use_global_device_ids=true | all-gather | bytes 655360 | tf_op jit(solution)/shard_map/while/body/eval_jaxpr/all_gather | solution.py:111
  426.0 1.0 copy-done
  427.0 53.1 %reduce-scatter.2.cloned.1.call-done = f32[32,2048]{1,0:T(8,128)} async-done(((f32[32,8192]{1,0:T(8,128)}), f32[32,2048]{1,0:T(8,128)}) %reduce-scatter.2.cloned.1.call-update) | async-done | bytes 262160 | tf_op jit(solution)/shard_map/while/body/eval_jaxpr/reduce_scatter | solution.py:113
  480.1 1.0 select_dynamic-update-slice_fusion.2
  481.1 1.3 collective-permute-start
  482.4 2.3 collective-permute-done
  485.6 13.5 %all_gather.27 = bf16[32,8192]{1,0:T(8,128)(2,1)S(1)} all-gather(bf16[32,2048]{1,0:T(8,128)(2,1)S(1)} %dynamic-slice_select_fusion.2), channel_id=1, replica_groups=mesh['replica'=2,'section'=4,'tensor'=4] {'tensor'}, dimensions={1}, use_global_device_ids=true | all-gather | bytes 655360 | tf_op jit(solution)/shard_map/while/body/eval_jaxpr/all_gather | solution.py:111
  499.2 1.0 copy-done
  500.2 57.4 %reduce-scatter.2.cloned.1.call-done = f32[32,2048]{1,0:T(8,128)} async-done(((f32[32,8192]{1,0:T(8,128)}), f32[32,2048]{1,0:T(8,128)}) %reduce-scatter.2.cloned.1.call-update) | async-done | bytes 262160 | tf_op jit(solution)/shard_map/while/body/eval_jaxpr/reduce_scatter | solution.py:113
  557.6 1.0 select_dynamic-update-slice_fusion.2
  558.6 1.3 collective-permute-start
  559.9 2.3 collective-permute-done
  563.1 13.4 %all_gather.27 = bf16[32,8192]{1,0:T(8,128)(2,1)S(1)} all-gather(bf16[32,2048]{1,0:T(8,128)(2,1)S(1)} %dynamic-slice_select_fusion.2), channel_id=1, replica_groups=mesh['replica'=2,'section'=4,'tensor'=4] {'tensor'}, dimensions={1}, use_global_device_ids=true | all-gather | bytes 655360 | tf_op jit(solution)/shard_map/while/body/eval_jaxpr/all_gather | solution.py:111
  576.5 26.1 %conditional.4 = (f32[32,8192]{1,0:T(8,128)S(1)}, bf16[128,512]{0,1:T(8,128)(2,1)S(1)}) conditional(s32[]{:T(128)} %convert_element_type.152, bf16[128,512]{0,1:T(8,128)(2,1)S(1)} %get-tuple-element.494, (bf16[32,8192]{1,0:T(8,128)(2,1)S(1)}, f32[1,8192]{1,0:T(1,128)S(1)}, bf16[8192,512]{1,0:T(8,128)(2,1)}, s32[]{:T(128)}, ...), branch_computations={%region_1.1_spmd, %region_2.5_spmd} | conditional | flops 1371679616 | bytes 48361408 | solution.py:112
  576.8 5.0 fusion.13
  582.8 8.8 %convolution_bitcast_fusion = f32[4,8,8,128]{3,1,2,0:T(8,128)S(1)} fusion(bf16[8192,1024]{1,0:T(8,128)(2,1)} %get-tuple-element.270, bf16[32,8192]{1,0:T(8,128)(2,1)S(1)} %get-tuple-element.263, f32[8192]{0:T(1024)S(1)} %bitcast.78, f32[32]{0:T(128)S(1)} %add_rsqrt_fusion), kind=kOutput, calls=%fused_computation.11 | convolution fusion | flops 537919488 | bytes 17465472 | tf_op jit(solution)/shard_map/while/body/eval_jaxpr/cond/branch_1_fun/dot_general | solution.py:67
  593.8 8.7 %convolution_convert_fusion = bf16[32,8192]{1,0:T(8,128)(2,1)S(1)} fusion(bf16[32,1024]{1,0:T(8,128)(2,1)S(1)} %reshape.193, bf16[1024,8192]{1,0:T(8,128)(2,1)} %get-tuple-element.271), kind=kOutput, calls=%fused_computation.2 | convolution fusion | flops 537133056 | bytes 17367040 | tf_op jit(solution)/shard_map/while/body/eval_jaxpr/cond/branch_1_fun/dot_general | solution.py:93
  603.6 31.9 %reduce-scatter.2.cloned.1.call-done = f32[32,2048]{1,0:T(8,128)} async-done(((f32[32,8192]{1,0:T(8,128)}), f32[32,2048]{1,0:T(8,128)}) %reduce-scatter.2.cloned.1.call-update) | async-done | bytes 262160 | tf_op jit(solution)/shard_map/while/body/eval_jaxpr/reduce_scatter | solution.py:113
  635.5 1.0 select_dynamic-update-slice_fusion.2
  636.5 1.3 collective-permute-start
  637.8 2.3 collective-permute-done
  641.0 13.5 %all_gather.27 = bf16[32,8192]{1,0:T(8,128)(2,1)S(1)} all-gather(bf16[32,2048]{1,0:T(8,128)(2,1)S(1)} %dynamic-slice_select_fusion.2), channel_id=1, replica_groups=mesh['replica'=2,'section'=4,'tensor'=4] {'tensor'}, dimensions={1}, use_global_device_ids=true | all-gather | bytes 655360 | tf_op jit(solution)/shard_map/while/body/eval_jaxpr/all_gather | solution.py:111
  654.5 26.5 %conditional.4 = (f32[32,8192]{1,0:T(8,128)S(1)}, bf16[128,512]{0,1:T(8,128)(2,1)S(1)}) conditional(s32[]{:T(128)} %convert_element_type.152, bf16[128,512]{0,1:T(8,128)(2,1)S(1)} %get-tuple-element.494, (bf16[32,8192]{1,0:T(8,128)(2,1)S(1)}, f32[1,8192]{1,0:T(1,128)S(1)}, bf16[8192,512]{1,0:T(8,128)(2,1)}, s32[]{:T(128)}, ...), branch_computations={%region_1.1_spmd, %region_2.5_spmd} | conditional | flops 1371679616 | bytes 48361408 | solution.py:112
  654.7 5.0 fusion.13
  661.2 8.8 %convolution_bitcast_fusion = f32[4,8,8,128]{3,1,2,0:T(8,128)S(1)} fusion(bf16[8192,1024]{1,0:T(8,128)(2,1)} %get-tuple-element.270, bf16[32,8192]{1,0:T(8,128)(2,1)S(1)} %get-tuple-element.263, f32[8192]{0:T(1024)S(1)} %bitcast.78, f32[32]{0:T(128)S(1)} %add_rsqrt_fusion), kind=kOutput, calls=%fused_computation.11 | convolution fusion | flops 537919488 | bytes 17465472 | tf_op jit(solution)/shard_map/while/body/eval_jaxpr/cond/branch_1_fun/dot_general | solution.py:67
  672.1 8.7 %convolution_convert_fusion = bf16[32,8192]{1,0:T(8,128)(2,1)S(1)} fusion(bf16[32,1024]{1,0:T(8,128)(2,1)S(1)} %reshape.193, bf16[1024,8192]{1,0:T(8,128)(2,1)} %get-tuple-element.271), kind=kOutput, calls=%fused_computation.2 | convolution fusion | flops 537133056 | bytes 17367040 | tf_op jit(solution)/shard_map/while/body/eval_jaxpr/cond/branch_1_fun/dot_general | solution.py:93
  681.0 1.0 copy-done
  682.0 31.4 %reduce-scatter.2.cloned.1.call-done = f32[32,2048]{1,0:T(8,128)} async-done(((f32[32,8192]{1,0:T(8,128)}), f32[32,2048]{1,0:T(8,128)}) %reduce-scatter.2.cloned.1.call-update) | async-done | bytes 262160 | tf_op jit(solution)/shard_map/while/body/eval_jaxpr/reduce_scatter | solution.py:113
  713.4 1.0 select_dynamic-update-slice_fusion.2
  714.4 1.3 collective-permute-start
  715.7 2.3 collective-permute-done
  718.9 13.5 %all_gather.27 = bf16[32,8192]{1,0:T(8,128)(2,1)S(1)} all-gather(bf16[32,2048]{1,0:T(8,128)(2,1)S(1)} %dynamic-slice_select_fusion.2), channel_id=1, replica_groups=mesh['replica'=2,'section'=4,'tensor'=4] {'tensor'}, dimensions={1}, use_global_device_ids=true | all-gather | bytes 655360 | tf_op jit(solution)/shard_map/while/body/eval_jaxpr/all_gather | solution.py:111
  732.5 26.5 %conditional.4 = (f32[32,8192]{1,0:T(8,128)S(1)}, bf16[128,512]{0,1:T(8,128)(2,1)S(1)}) conditional(s32[]{:T(128)} %convert_element_type.152, bf16[128,512]{0,1:T(8,128)(2,1)S(1)} %get-tuple-element.494, (bf16[32,8192]{1,0:T(8,128)(2,1)S(1)}, f32[1,8192]{1,0:T(1,128)S(1)}, bf16[8192,512]{1,0:T(8,128)(2,1)}, s32[]{:T(128)}, ...), branch_computations={%region_1.1_spmd, %region_2.5_spmd} | conditional | flops 1371679616 | bytes 48361408 | solution.py:112
  732.7 5.0 fusion.13
  739.2 8.8 %convolution_bitcast_fusion = f32[4,8,8,128]{3,1,2,0:T(8,128)S(1)} fusion(bf16[8192,1024]{1,0:T(8,128)(2,1)} %get-tuple-element.270, bf16[32,8192]{1,0:T(8,128)(2,1)S(1)} %get-tuple-element.263, f32[8192]{0:T(1024)S(1)} %bitcast.78, f32[32]{0:T(128)S(1)} %add_rsqrt_fusion), kind=kOutput, calls=%fused_computation.11 | convolution fusion | flops 537919488 | bytes 17465472 | tf_op jit(solution)/shard_map/while/body/eval_jaxpr/cond/branch_1_fun/dot_general | solution.py:67
  750.1 8.7 %convolution_convert_fusion = bf16[32,8192]{1,0:T(8,128)(2,1)S(1)} fusion(bf16[32,1024]{1,0:T(8,128)(2,1)S(1)} %reshape.193, bf16[1024,8192]{1,0:T(8,128)(2,1)} %get-tuple-element.271), kind=kOutput, calls=%fused_computation.2 | convolution fusion | flops 537133056 | bytes 17367040 | tf_op jit(solution)/shard_map/while/body/eval_jaxpr/cond/branch_1_fun/dot_general | solution.py:93
  760.0 31.4 %reduce-scatter.2.cloned.1.call-done = f32[32,2048]{1,0:T(8,128)} async-done(((f32[32,8192]{1,0:T(8,128)}), f32[32,2048]{1,0:T(8,128)}) %reduce-scatter.2.cloned.1.call-update) | async-done | bytes 262160 | tf_op jit(solution)/shard_map/while/body/eval_jaxpr/reduce_scatter | solution.py:113
  791.3 1.0 select_dynamic-update-slice_fusion.2
  792.3 1.3 collective-permute-start
  793.6 2.3 collective-permute-done
  796.9 13.4 %all_gather.27 = bf16[32,8192]{1,0:T(8,128)(2,1)S(1)} all-gather(bf16[32,2048]{1,0:T(8,128)(2,1)S(1)} %dynamic-slice_select_fusion.2), channel_id=1, replica_groups=mesh['replica'=2,'section'=4,'tensor'=4] {'tensor'}, dimensions={1}, use_global_device_ids=true | all-gather | bytes 655360 | tf_op jit(solution)/shard_map/while/body/eval_jaxpr/all_gather | solution.py:111
  810.2 26.5 %conditional.4 = (f32[32,8192]{1,0:T(8,128)S(1)}, bf16[128,512]{0,1:T(8,128)(2,1)S(1)}) conditional(s32[]{:T(128)} %convert_element_type.152, bf16[128,512]{0,1:T(8,128)(2,1)S(1)} %get-tuple-element.494, (bf16[32,8192]{1,0:T(8,128)(2,1)S(1)}, f32[1,8192]{1,0:T(1,128)S(1)}, bf16[8192,512]{1,0:T(8,128)(2,1)}, s32[]{:T(128)}, ...), branch_computations={%region_1.1_spmd, %region_2.5_spmd} | conditional | flops 1371679616 | bytes 48361408 | solution.py:112
  810.5 5.0 fusion.13
  817.0 8.8 %convolution_bitcast_fusion = f32[4,8,8,128]{3,1,2,0:T(8,128)S(1)} fusion(bf16[8192,1024]{1,0:T(8,128)(2,1)} %get-tuple-element.270, bf16[32,8192]{1,0:T(8,128)(2,1)S(1)} %get-tuple-element.263, f32[8192]{0:T(1024)S(1)} %bitcast.78, f32[32]{0:T(128)S(1)} %add_rsqrt_fusion), kind=kOutput, calls=%fused_computation.11 | convolution fusion | flops 537919488 | bytes 17465472 | tf_op jit(solution)/shard_map/while/body/eval_jaxpr/cond/branch_1_fun/dot_general | solution.py:67
  827.9 8.7 %convolution_convert_fusion = bf16[32,8192]{1,0:T(8,128)(2,1)S(1)} fusion(bf16[32,1024]{1,0:T(8,128)(2,1)S(1)} %reshape.193, bf16[1024,8192]{1,0:T(8,128)(2,1)} %get-tuple-element.271), kind=kOutput, calls=%fused_computation.2 | convolution fusion | flops 537133056 | bytes 17367040 | tf_op jit(solution)/shard_map/while/body/eval_jaxpr/cond/branch_1_fun/dot_general | solution.py:93
  837.8 25.1 %reduce-scatter.2.cloned.1.call-done = f32[32,2048]{1,0:T(8,128)} async-done(((f32[32,8192]{1,0:T(8,128)}), f32[32,2048]{1,0:T(8,128)}) %reduce-scatter.2.cloned.1.call-update) | async-done | bytes 262160 | tf_op jit(solution)/shard_map/while/body/eval_jaxpr/reduce_scatter | solution.py:113
  862.9 1.0 select_dynamic-update-slice_fusion.2
  863.9 1.3 collective-permute-start
  865.2 2.3 collective-permute-done
  (169 shorter events, 29.5 us)
Async XLA Ops:
  7.2 107.6 %all-gather.3.cloned.1.call-start = ((), (), s32[]{:S(2)}) async-start(), calls=%async_computation.1 | async-start | bytes 12582912 | tf_op jit(solution)/shard_map/all_gather | solution.py:47
  7.9 307.4 %all-gather.5.cloned.1.call-start = ((), (), s32[]{:S(2)}) async-start(), calls=%async_computation.2 | async-start | bytes 25165824 | tf_op jit(solution)/shard_map/all_gather | solution.py:45
  114.8 2.8 slice-start
  114.8 3.5 slice-start.1
  318.0 18.1 %copy-start.1 = (f32[1,8192]{1,0:T(1,128)S(1)}, f32[1,8192]{1,0:T(1,128)}, u32[]{:S(2)}) copy-start(f32[1,8192]{1,0:T(1,128)} %param.14) | copy-start | bytes 98308
  336.1 70.8 %reduce-scatter.2.cloned.1.call-start = ((), (), s32[]{:S(2)}) async-start(), calls=%async_computation.3 | async-start | bytes 1310720 | tf_op jit(solution)/shard_map/while/body/eval_jaxpr/reduce_scatter | solution.py:113
  351.4 1.0 copy-start
  407.9 3.6 collective-permute-start
  411.5 68.6 %reduce-scatter.2.cloned.1.call-start = ((), (), s32[]{:S(2)}) async-start(), calls=%async_computation.3 | async-start | bytes 1310720 | tf_op jit(solution)/shard_map/while/body/eval_jaxpr/reduce_scatter | solution.py:113
  426.0 1.0 copy-start
  481.1 3.6 collective-permute-start
  484.7 72.9 %reduce-scatter.2.cloned.1.call-start = ((), (), s32[]{:S(2)}) async-start(), calls=%async_computation.3 | async-start | bytes 1310720 | tf_op jit(solution)/shard_map/while/body/eval_jaxpr/reduce_scatter | solution.py:113
  499.2 1.0 copy-start
  558.6 3.6 collective-permute-start
  562.2 73.3 %reduce-scatter.2.cloned.1.call-start = ((), (), s32[]{:S(2)}) async-start(), calls=%async_computation.3 | async-start | bytes 1310720 | tf_op jit(solution)/shard_map/while/body/eval_jaxpr/reduce_scatter | solution.py:113
  602.6 1.0 copy-start
  636.5 3.6 collective-permute-start
  640.1 73.3 %reduce-scatter.2.cloned.1.call-start = ((), (), s32[]{:S(2)}) async-start(), calls=%async_computation.3 | async-start | bytes 1310720 | tf_op jit(solution)/shard_map/while/body/eval_jaxpr/reduce_scatter | solution.py:113
  681.0 1.0 copy-start
  714.4 3.6 collective-permute-start
  718.0 73.3 %reduce-scatter.2.cloned.1.call-start = ((), (), s32[]{:S(2)}) async-start(), calls=%async_computation.3 | async-start | bytes 1310720 | tf_op jit(solution)/shard_map/while/body/eval_jaxpr/reduce_scatter | solution.py:113
  759.0 1.0 copy-start
  792.3 3.6 collective-permute-start
  795.9 67.0 %reduce-scatter.2.cloned.1.call-start = ((), (), s32[]{:S(2)}) async-start(), calls=%async_computation.3 | async-start | bytes 1310720 | tf_op jit(solution)/shard_map/while/body/eval_jaxpr/reduce_scatter | solution.py:113
  836.7 1.0 copy-start
  863.9 3.6 collective-permute-start
  867.5 0.8 copy-start.2
Sparse Core Ops, SparseCore 0:
  9.5 105.2 all-gather.2
  116.4 198.8 all-gather.4
  352.5 54.2 reduce-scatter.1
  427.1 52.9 reduce-scatter.1
  500.3 57.2 reduce-scatter.1
  603.7 31.6 reduce-scatter.1
  682.1 31.2 reduce-scatter.1
  760.1 31.1 reduce-scatter.1
  837.9 24.9 reduce-scatter.1
where the time goes:
time: 879 us; the launch traced here: 875 us
  waiting for transfers between devices  590 us (67%)
  blocking collectives  101 us (11%)
  matrix products  94.6 us (11%)
  other arithmetic  44.2 us (5%)
  local copies, waits for them, and re-layouts  20.1 us (2%)
  between operations  13.8 us (2%)
  starting transfers between devices  9.18 us (1%)
    reduce_scatter x7, waiting for transfers between devices, tick(): lax.psum_scatter(partial_value, 'tensor', scatter_dimension=1, tiled=True)  285 us
    all_gather x1, waiting for transfers between devices, per_device(): lax.all_gather(q_tiles, 'replica', axis=1, tiled=True)  190 us
    all_gather x1, waiting for transfers between devices, per_device(): lax.all_gather(kv_tiles, 'replica', axis=1, tiled=True)  98 us
    all_gather x7, blocking collectives, tick(): full = lax.all_gather(current, 'tensor', axis=1, tiled=True)  94.9 us
    dot_general x4, matrix products, layer_block(): jnp.dot(normed, w_query, preferred_element_type=jnp.float32)  35.3 us
    dot_general x4, matrix products, layer_block(): partial_value = jnp.dot(attended, w_out, preferred_element_type=jnp.float32)  35 us
    convert_element_type x2, other arithmetic, dequantize(): return scaled.reshape(rows, cols).astype(jnp.bfloat16)  24.6 us
    dot_general x4, matrix products, layer_block(): jnp.dot(normed, w_keyval, preferred_element_type=jnp.float32)  19.9 us
  transfers between devices with their start and end apart: 16, of which 16 were waited for; matrix products, arithmetic and copies ran while one was open for 1% of the time, Pallas kernels for 0%

commit v1 on v0

v1 whole, which is shorter than its diff:
```python
import functools

import jax
import jax.numpy as jnp
from jax import lax
from jax.experimental import pallas as pl
from jax.experimental.pallas import tpu as pltpu
from jax.sharding import PartitionSpec as P

HEAD = 128
BLOCK = 128
N_TILE = 256
OUT_TILE = 512
STRIP = 16

rope_base = 1000000.0
norm_eps = 1e-06

AXES = ("replica", "section", "tensor")
VMEM_LIMIT = 48 * 1024 * 1024


def project_kernel(pieces, replicas, q_steps, kv_steps, place, *refs):
    blocks = refs[:pieces]
    gain, q_tile, kv_tile, scale, out, held, square, weight = refs[pieces:]
    rows, width = blocks[0].shape
    step = pl.program_id(0)
    columns = pl.ds(pl.multiple_of(step * N_TILE, N_TILE), N_TILE)

    @pl.when(step == 0)
    def _():
        square[...] = jnp.zeros_like(square)
        for index, block in enumerate(blocks):
            slot = lax.rem(place[0] + pieces - index, pieces)
            top = lax.rem(slot, replicas) * rows
            left = lax.div(slot, replicas) * width
            span = pl.ds(pl.multiple_of(left, HEAD), width)

            def strip(number, _):
                source = pl.ds(pl.multiple_of(number * STRIP, STRIP), STRIP)
                target = pl.ds(pl.multiple_of(top + number * STRIP, STRIP), STRIP)
                values = block[source, :].astype(jnp.float32)
                held[target, span] = (values * gain[:, span]).astype(jnp.bfloat16)
                square[target, :] += jnp.sum(values * values, -1, keepdims=True)
                return 0

            lax.fori_loop(0, rows // STRIP, strip, 0)
        for replica in range(replicas):
            total = square[replica * rows:(replica + 1) * rows, :]
            coarse = total.astype(jnp.bfloat16)
            rest = (total - coarse.astype(jnp.float32)).astype(jnp.bfloat16)
            lane = lax.broadcasted_iota(jnp.int32, total.shape, 1)
            pair = jnp.where(lane < HEAD // 2, coarse.astype(jnp.float32), rest.astype(jnp.float32))
            out[replica, :, pl.ds((q_steps + kv_steps) * N_TILE, HEAD)] = pair.astype(jnp.bfloat16)

    def rescale(tile):
        for number in range(tile.shape[0] // BLOCK):
            span = pl.ds(number * BLOCK, BLOCK)
            factor = jnp.broadcast_to(scale[pl.ds(number, 1), columns], (BLOCK, N_TILE))
            weight[span, :] = (tile[span, :].astype(jnp.float32) * factor).astype(jnp.bfloat16)

    pl.when(step < q_steps)(lambda: rescale(q_tile))
    pl.when(step >= q_steps)(lambda: rescale(kv_tile))
    for replica in range(replicas):
        share = held[replica * rows:(replica + 1) * rows, :]
        product = jnp.dot(share, weight[...], preferred_element_type=jnp.float32)
        out[replica, :, columns] = product.astype(jnp.bfloat16)


def project(pieces, place, gain, q_tiles, kv_tiles, scales, replicas):
    rows, width = pieces[0].shape
    depth, q_cols = q_tiles.shape
    kv_cols = kv_tiles.shape[1]
    q_steps, kv_steps = q_cols // N_TILE, kv_cols // N_TILE
    total = q_cols + kv_cols + HEAD
    whole = lambda *shape: pl.BlockSpec(shape, lambda j, place: (0,) * len(shape))
    return pl.pallas_call(
        functools.partial(project_kernel, len(pieces), replicas, q_steps, kv_steps),
        grid_spec=pltpu.PrefetchScalarGridSpec(
            num_scalar_prefetch=1,
            grid=(q_steps + kv_steps,),
            in_specs=[whole(rows, width)] * len(pieces)
            + [
                whole(1, depth),
                pl.BlockSpec((depth, N_TILE), lambda j, place: (0, jnp.minimum(j, q_steps - 1))),
                pl.BlockSpec((depth, N_TILE), lambda j, place: (0, jnp.maximum(j - q_steps, 0))),
                whole(*scales.shape),
            ],
            out_specs=whole(replicas, rows, total),
            scratch_shapes=[
                pltpu.VMEM((replicas * rows, depth), jnp.bfloat16),
                pltpu.VMEM((replicas * rows, HEAD), jnp.float32),
                pltpu.VMEM((depth, N_TILE), jnp.bfloat16),
            ],
        ),
        out_shape=jax.ShapeDtypeStruct((replicas, rows, total), jnp.bfloat16),
        compiler_params=pltpu.CompilerParams(vmem_limit_bytes=VMEM_LIMIT),
        name="project",
    )(place, *pieces, gain, q_tiles, kv_tiles, scales)


def attend_kernel(q_heads, kv_heads, features, length, parts, cosine, sine, out, cache):
    replicas, rows, _ = parts.shape
    group = q_heads // kv_heads

    def total(start):
        value = parts[0, :, start:start + HEAD].astype(jnp.float32)
        for other in range(1, replicas):
            value = value + parts[other, :, start:start + HEAD].astype(jnp.float32)
        return value

    pair = total((q_heads + 2 * kv_heads) * HEAD)
    square = pair[:, :1] + pair[:, HEAD // 2:HEAD // 2 + 1]
    factor = jnp.broadcast_to(lax.rsqrt(square / features + norm_eps), (rows, HEAD))

    def rotate(value):
        return value * cosine[...] + pltpu.roll(value, HEAD // 2, 1) * sine[...]

    row = lax.broadcasted_iota(jnp.int32, (rows, rows), 0)
    col = lax.broadcasted_iota(jnp.int32, (rows, rows), 1)
    mask = jnp.concatenate([(col <= row) & (col < length[0])] * group, 0)
    for kv_head in range(kv_heads):
        start = (q_heads + 2 * kv_head) * HEAD
        keys = rotate(total(start) * factor).astype(jnp.bfloat16)
        values = (total(start + HEAD) * factor).astype(jnp.bfloat16)
        cache[:, 2 * kv_head * HEAD:(2 * kv_head + 1) * HEAD] = keys
        cache[:, (2 * kv_head + 1) * HEAD:(2 * kv_head + 2) * HEAD] = values
        heads = range(kv_head * group, (kv_head + 1) * group)
        query = jnp.concatenate(
            [rotate(total(head * HEAD) * factor).astype(jnp.bfloat16) for head in heads], 0
        )
        scores = lax.dot_general(
            query, keys, (((1,), (1,)), ((), ())), preferred_element_type=jnp.float32
        )
        scores = jnp.where(mask, scores / jnp.sqrt(jnp.float32(HEAD)), -jnp.inf)
        expo = jnp.exp(scores - jnp.max(scores, -1, keepdims=True))
        probs = (expo / jnp.sum(expo, -1, keepdims=True)).astype(jnp.bfloat16)
        mixed = jnp.dot(probs, values, preferred_element_type=jnp.float32).astype(jnp.bfloat16)
        for number, head in enumerate(heads):
            out[:, head * HEAD:(head + 1) * HEAD] = mixed[number * rows:(number + 1) * rows, :]


def attend(parts, length, cosine, sine, q_cols, kv_cols, features):
    rows = parts.shape[1]
    vmem = pl.BlockSpec(memory_space=pltpu.VMEM)
    return pl.pallas_call(
        functools.partial(attend_kernel, q_cols // HEAD, kv_cols // (2 * HEAD), features),
        in_specs=[pl.BlockSpec(memory_space=pltpu.SMEM), vmem, vmem, vmem],
        out_specs=[vmem, vmem],
        out_shape=[
            jax.ShapeDtypeStruct((rows, q_cols), jnp.bfloat16),
            jax.ShapeDtypeStruct((rows, kv_cols), jnp.bfloat16),
        ],
        compiler_params=pltpu.CompilerParams(vmem_limit_bytes=VMEM_LIMIT),
        name="attend",
    )(length, parts, cosine, sine)


def spread_kernel(attended, weight, out):
    product = jnp.dot(attended[...], weight[...], preferred_element_type=jnp.float32)
    out[...] = product.astype(jnp.bfloat16)


def spread(attended, weight, shards):
    rows, depth = attended.shape
    width = weight.shape[1] // shards
    tile = min(OUT_TILE, width)
    per = width // tile
    return pl.pallas_call(
        spread_kernel,
        grid=(shards * per,),
        in_specs=[
            pl.BlockSpec((rows, depth), lambda j: (0, 0)),
            pl.BlockSpec((depth, tile), lambda j: (0, j)),
        ],
        out_specs=pl.BlockSpec((None, rows, tile), lambda j: (j // per, 0, j % per)),
        out_shape=jax.ShapeDtypeStruct((shards, rows, width), jnp.bfloat16),
        compiler_params=pltpu.CompilerParams(vmem_limit_bytes=VMEM_LIMIT),
        name="spread",
    )(attended, weight)


def per_device(sizes, hidden_in, lengths, norm_gain, q_tiles, q_scales, kv_tiles, kv_scales, out_weight):
    replicas, sections, shards = sizes
    section = lax.axis_index("section")
    rows, width = hidden_in.shape
    features = norm_gain.shape[1]
    q_tiles, kv_tiles, w_out = q_tiles[0], kv_tiles[0], out_weight[0]
    depth, q_cols = q_tiles.shape
    kv_cols = kv_tiles.shape[1]
    per_slice = shards // replicas
    place = lax.axis_index("tensor").astype(jnp.int32)[None]
    gain = lax.dynamic_slice_in_dim(norm_gain, lax.axis_index("replica") * depth, depth, 1)
    scales = jnp.repeat(jnp.concatenate([q_scales[0], kv_scales[0]], 1).astype(jnp.float32), BLOCK, 1)
    half = HEAD // 2
    freq = rope_base ** (-jnp.arange(half, dtype=jnp.float32) / half)
    angle = jnp.arange(rows, dtype=jnp.float32)[:, None] * freq[None, :]
    cosine = jnp.concatenate([jnp.cos(angle)] * 2, 1)
    sine = jnp.concatenate([-jnp.sin(angle), jnp.sin(angle)], 1)

    def device(replica, sect, shard):
        return (replica * sections + sect) * shards + shard

    def gather(value, source_of, target):
        pieces = []
        for turn in range(shards):
            pairs = []
            for replica in range(replicas):
                for shard in range(shards):
                    goal = ((shard % per_slice) * replicas + replica + turn) % shards
                    pairs.append(
                        (
                            device(replica, source_of(turn), shard),
                            device(shard // per_slice, target, goal),
                        )
                    )
            pieces.append(lax.ppermute(value, AXES, pairs))
        return pieces

    hidden = hidden_in
    layer_out = jnp.zeros((rows, width), jnp.bfloat16)
    cache_out = jnp.zeros((rows, kv_cols), jnp.bfloat16)
    for layer in range(sections):
        if layer == 0:
            pieces = gather(hidden, lambda turn: turn % sections, 0)
            residual = hidden
        else:
            pieces = gather(layer_out, lambda turn: layer - 1, layer)
            pairs = [
                (device(replica, layer - 1, shard), device(replica, layer, shard))
                for replica in range(replicas)
                for shard in range(shards)
            ]
            residual = lax.ppermute(layer_out, AXES, pairs)

        def work(pieces, residual, layer_out, cache_out):
            parts = project(pieces, place, gain, q_tiles, kv_tiles, scales, replicas)
            parts = lax.all_to_all(parts, "replica", 0, 0, tiled=True)
            attended, cache = attend(parts, lengths, cosine, sine, q_cols, kv_cols, features)
            partials = spread(attended, w_out, shards)
            partials = lax.all_to_all(partials, "tensor", 0, 0, tiled=True)
            total = residual.astype(jnp.float32) + jnp.sum(partials.astype(jnp.float32), 0)
            return total.astype(jnp.bfloat16), cache

        def rest(pieces, residual, layer_out, cache_out):
            return layer_out, cache_out

        layer_out, cache_out = lax.cond(
            section == layer, work, rest, pieces, residual, layer_out, cache_out
        )
    return layer_out[None], cache_out[None]


def solution(mesh):
    sizes = tuple(mesh.shape[axis] for axis in AXES)
    in_specs = (
        P("replica", "tensor"),
        P("replica"),
        P("section", None),
        P("section", "replica", "tensor"),
        P("section", "replica", "tensor"),
        P("section", "replica", "tensor"),
        P("section", "replica", "tensor"),
        P("section", "tensor", None),
    )
    out_specs = (P("section", "replica", "tensor"), P("section", "replica", "tensor"))
    return jax.shard_map(
        functools.partial(per_device, sizes),
        mesh=mesh,
        in_specs=in_specs,
        out_specs=out_specs,
        check_vma=False,
    )
```

time: 879 us -> 390 us (0.44)
  waiting for transfers between devices: 590 us -> 286 us
  matrix products: 94.6 us -> 0 us
  blocking collectives: 101 us -> 44.7 us
  other arithmetic: 44.2 us -> 2.36 us
  Pallas kernels: 0 us -> 28.5 us
  local copies, waits for them, and re-layouts: 20.1 us -> 1.77 us
  starting transfers between devices: 9.18 us -> 25.1 us
  between operations: 13.8 us -> 1 us
    all_gather x2 -> x0, waiting for transfers between devices: 288 us -> none  [the longest x1 190 us: per_device(): lax.all_gather(q_tiles, 'replica', axis=1, tiled=True)]
    reduce_scatter x7 -> x0, waiting for transfers between devices: 285 us -> none  [tick(): lax.psum_scatter(partial_value, 'tensor', scatter_dimension=1, tiled=True)]
    ppermute x7 -> x19, waiting for transfers between devices: 16 us -> 286 us  [the longest x3 259 us: per_device(): residual = lax.ppermute(layer_out, AXES, pairs)]
    all_gather x9 -> x0, blocking collectives: 101 us -> none  [the longest x7 94.9 us: tick(): full = lax.all_gather(current, 'tensor', axis=1, tiled=True)]
    dot_general x20 -> x0, matrix products: 93 us -> none  [the longest x4 35.3 us: layer_block(): jnp.dot(normed, w_query, preferred_element_type=jnp.float32)]
    all_to_all x0 -> x2, blocking collectives: none -> 44.7 us  [the longest x1 31.1 us: work(): partials = lax.all_to_all(partials, 'tensor', 0, 0, tiled=True)]
    pallas_call x0 -> x3, Pallas kernels: none -> 28.5 us  [the longest x1 13.6 us: spread(): pl.pallas_call(spread_kernel, grid=(shards * per,), in_specs=[pl.BlockSpe...]
    convert_element_type x8 -> x1, other arithmetic: 25 us -> 0.71 us  [per_device(): jnp.concatenate([q_scales[0], kv_scales[0]], 1).astype(jnp.float32)]
  transfers between devices with their start and end apart: 16 -> 19, of which waited for: 16 -> 5; matrix products, arithmetic and copies ran while one was open for 1% -> 0% of each run, Pallas kernels for 0% -> 0%
where the time goes in v1:
time: 390 us; the launch traced here: 389 us
  waiting for transfers between devices  286 us (73%)
  blocking collectives  44.7 us (11%)
  Pallas kernels  28.5 us (7%)
  starting transfers between devices  25.1 us (6%)
    ppermute x3, waiting for transfers between devices, per_device(): residual = lax.ppermute(layer_out, AXES, pairs)  259 us
    all_to_all x1, blocking collectives, work(): partials = lax.all_to_all(partials, 'tensor', 0, 0, tiled=True)  31.1 us
    ppermute x16, waiting for transfers between devices, gather(): pieces.append(lax.ppermute(value, AXES, pairs))  26.4 us
    ppermute x16, starting transfers between devices, gather(): pieces.append(lax.ppermute(value, AXES, pairs))  22.4 us
    pallas_call x1, Pallas kernels, spread(): pl.pallas_call(spread_kernel, grid=(shards * per,), in_specs=[pl.BlockSpe...  13.6 us
    all_to_all x1, blocking collectives, work(): parts = lax.all_to_all(parts, 'replica', 0, 0, tiled=True)  13.6 us
    pallas_call x1, Pallas kernels, project(): pl.pallas_call(functools.partial(project_kernel, len(pieces), replicas, q...  13.2 us
  transfers between devices with their start and end apart: 19, of which 5 were waited for; matrix products, arithmetic and copies ran while one was open for 0% of the time, Pallas kernels for 0%

profile of v1, /device:TPU:3, one launch (start us, length us, event | category | flops | bytes accessed | tf_op | source)
XLA Modules:
  0.0 389.4 jit_solution(15935632810926102169)
XLA Ops:
  0.6 0.0 copy-start
  0.6 0.7 collective-permute-start
  1.3 0.7 collective-permute-start.1
  2.0 0.7 collective-permute-start.2
  2.8 9.6 %collective-permute-start.3 = (bf16[128,2048]{1,0:T(8,128)(2,1)}, bf16[128,2048]{1,0:T(8,128)(2,1)S(1)}, u32[]{:S(2)}, u32[]{:S(2)}) collective-permute-start(bf16[128,2048]{1,0:T(8,128)(2,1)} %param.16), channel_id=1, source_target_pairs={{12,3},{13,1},{14,19},{15,17},{28,0},{29,2},{30,16},{31,18}} | collective-permute-start | bytes 1572872 | tf_op jit(solution)/shard_map/ppermute | solution.py:217
  12.4 0.3 fusion.3
  12.7 0.7 maximum_convert_fusion
  13.4 0.1 copy.11
  13.5 0.1 broadcast_in_dim.29
  13.6 0.1 copy.14
  13.7 0.1 pad_maximum_fusion
  13.8 0.0 copy-done
  13.8 0.0 collective-permute-done
  13.8 0.0 collective-permute-done.1
  13.8 0.0 collective-permute-done.2
  13.8 8.7 %collective-permute-done.3 = bf16[128,2048]{1,0:T(8,128)(2,1)S(1)} collective-permute-done((bf16[128,2048]{1,0:T(8,128)(2,1)}, bf16[128,2048]{1,0:T(8,128)(2,1)S(1)}, u32[]{:S(2)}, u32[]{:S(2)}) %collective-permute-start.3) | collective-permute-done | bytes 524320 | tf_op jit(solution)/shard_map/ppermute | solution.py:217
  22.5 0.7 conditional.4
  22.6 0.7 broadcast_in_dim.21
  23.2 0.7 collective-permute-start.4
  23.9 0.7 collective-permute-start.5
  24.6 0.7 collective-permute-start.6
  25.3 0.7 collective-permute-start.7
  26.0 0.7 collective-permute-start.8
  26.8 0.0 collective-permute-done.4
  26.8 0.0 collective-permute-done.5
  26.8 0.0 collective-permute-done.6
  26.8 0.0 collective-permute-done.7
  26.8 0.0 collective-permute-done.8
  26.8 0.7 collective-permute-start.10
  27.5 0.7 collective-permute-start.11
  28.2 0.7 collective-permute-start.12
  28.9 0.7 collective-permute-start.13
  29.6 0.7 collective-permute-start.9
  30.3 0.0 collective-permute-done.10
  30.3 0.0 collective-permute-done.11
  30.4 0.0 collective-permute-done.12
  30.4 0.0 collective-permute-done.13
  30.4 0.0 collective-permute-done.9
  30.4 0.2 conditional.6
  30.6 0.0 copy-start.2
  30.6 1.3 collective-permute-start.14
  31.9 1.3 collective-permute-start.15
  33.2 1.3 collective-permute-start.16
  34.5 1.3 collective-permute-start.17
  35.8 1.3 collective-permute-start.18
  37.1 259.4 %collective-permute-done.14 = bf16[128,2048]{1,0:T(8,128)(2,1)S(1)} collective-permute-done((bf16[128,2048]{1,0:T(8,128)(2,1)S(1)}, bf16[128,2048]{1,0:T(8,128)(2,1)S(1)}, u32[]{:S(2)}, u32[]{:S(2)}) %collective-permute-start.14) | collective-permute-done | bytes 524320 | tf_op jit(solution)/shard_map/ppermute | solution.py:234
  296.5 1.3 collective-permute-done.15
  297.9 11.8 %collective-permute-done.16 = bf16[128,2048]{1,0:T(8,128)(2,1)S(1)} collective-permute-done((bf16[128,2048]{1,0:T(8,128)(2,1)S(1)}, bf16[128,2048]{1,0:T(8,128)(2,1)S(1)}, u32[]{:S(2)}, u32[]{:S(2)}) %collective-permute-start.16) | collective-permute-done | bytes 524320 | tf_op jit(solution)/shard_map/ppermute | solution.py:217
  309.7 4.5 %collective-permute-done.17 = bf16[128,2048]{1,0:T(8,128)(2,1)S(1)} collective-permute-done((bf16[128,2048]{1,0:T(8,128)(2,1)S(1)}, bf16[128,2048]{1,0:T(8,128)(2,1)S(1)}, u32[]{:S(2)}, u32[]{:S(2)}) %collective-permute-start.17) | collective-permute-done | bytes 524320 | tf_op jit(solution)/shard_map/ppermute | solution.py:217
  314.2 0.0 collective-permute-done.18
  314.2 0.0 copy-done.2
  314.2 74.5 %conditional.7 = (bf16[1,128,2048]{2,1,0:T(8,128)(2,1)}, bf16[1,128,512]{2,1,0:T(8,128)(2,1)}) conditional(s32[]{:T(128)} %convert_element_type.51, (bf16[128,2048]{1,0:T(8,128)(2,1)}, bf16[128,512]{1,0:T(8,128)(2,1)}) %tuple.82, (bf16[128,2048]{1,0:T(8,128)(2,1)S(1)}, s32[1]{0:T(128)}, bf16[128,2048]{1,0:T(8,128)(2,1)S(1)}, ...), branch_computations={%region_9.0_spmd, %region_10.0_spmd} | conditional | flops 2621440 | bytes 11141136 | solution.py:248
  314.2 13.2 %project.7 = bf16[2,128,1664]{2,1,0:T(8,128)(2,1)S(1)} custom-call(s32[1]{0:T(128)} %get-tuple-element.180.place, bf16[128,2048]{1,0:T(8,128)(2,1)S(1)} %get-tuple-element.181.refs_0_, bf16[128,2048]{1,0:T(8,128)(2,1)S(1)} %get-tuple-element.182.refs_1_, bf16[128,2048]{1,0:T(8,128)(2,1)S(1)} %get-tuple-element.183.refs_2_, ...), custom_call_target="tpu_custom_call" | custom-call | tf_op jit(solution)/shard_map/cond/branch_1_fun/project/pallas_call | solution.py:77
  327.4 13.6 %all_to_all.38.parts = bf16[2,128,1664]{2,1,0:T(8,128)(2,1)S(1)} all-to-all(bf16[2,128,1664]{2,1,0:T(8,128)(2,1)S(1)} %project.7), channel_id=1, replica_groups=mesh['replica'=2,'section'=4,'tensor'=4] {'replica'}, dimensions={0} | all-to-all | bytes 1703936 | tf_op jit(solution)/shard_map/cond/branch_1_fun/all_to_all | solution.py:238
  341.0 1.7 attend.7
  342.7 13.6 %spread.7 = bf16[4,128,2048]{2,1,0:T(8,128)(2,1)S(1)} custom-call(bf16[128,1024]{1,0:T(8,128)(2,1)S(1)} %get-tuple-element.191.attended, bf16[1024,8192]{1,0:T(8,128)(2,1)} %get-tuple-element.192.weight), custom_call_target="tpu_custom_call" | custom-call | tf_op jit(solution)/shard_map/cond/branch_1_fun/spread/pallas_call | solution.py:169
  356.3 31.1 %all_to_all.39 = bf16[4,128,2048]{2,1,0:T(8,128)(2,1)S(1)} all-to-all(bf16[4,128,2048]{2,1,0:T(8,128)(2,1)S(1)} %spread.7), channel_id=1, replica_groups=mesh['replica'=2,'section'=4,'tensor'=4] {'tensor'}, dimensions={0} | all-to-all | bytes 4194304 | tf_op jit(solution)/shard_map/cond/branch_1_fun/all_to_all | solution.py:241
  387.4 0.4 convert_reduce_fusion.3
  387.8 0.9 fusion
  388.7 0.0 copy-start.1
  388.7 0.8 copy-done.1
  (4 shorter events, 0.1 us)
Async XLA Ops:
  0.6 13.1 %copy-start = (f32[1,8192]{1,0:T(1,128)S(1)}, f32[1,8192]{1,0:T(1,128)}, u32[]{:S(2)}) copy-start(f32[1,8192]{1,0:T(1,128)} %param.18) | copy-start | bytes 98308
  0.6 13.2 %collective-permute-start = (bf16[128,2048]{1,0:T(8,128)(2,1)}, bf16[128,2048]{1,0:T(8,128)(2,1)S(1)}, u32[]{:S(2)}, u32[]{:S(2)}) collective-permute-start(bf16[128,2048]{1,0:T(8,128)(2,1)} %param.16), channel_id=1, source_target_pairs={{0,0},{1,2},{2,16},{3,18},{16,1},{17,3},{18,17},{19,19}} | collective-permute-start | bytes 1572872 | tf_op jit(solution)/shard_map/ppermute | solution.py:217
  1.3 12.5 %collective-permute-start.1 = (bf16[128,2048]{1,0:T(8,128)(2,1)}, bf16[128,2048]{1,0:T(8,128)(2,1)S(1)}, u32[]{:S(2)}, u32[]{:S(2)}) collective-permute-start(bf16[128,2048]{1,0:T(8,128)(2,1)} %param.16), channel_id=1, source_target_pairs={{4,1},{5,3},{6,17},{7,19},{20,2},{21,0},{22,18},{23,16}} | collective-permute-start | bytes 1572872 | tf_op jit(solution)/shard_map/ppermute | solution.py:217
  2.0 11.8 %collective-permute-start.2 = (bf16[128,2048]{1,0:T(8,128)(2,1)}, bf16[128,2048]{1,0:T(8,128)(2,1)S(1)}, u32[]{:S(2)}, u32[]{:S(2)}) collective-permute-start(bf16[128,2048]{1,0:T(8,128)(2,1)} %param.16), channel_id=1, source_target_pairs={{8,2},{9,0},{10,18},{11,16},{24,3},{25,1},{26,19},{27,17}} | collective-permute-start | bytes 1572872 | tf_op jit(solution)/shard_map/ppermute | solution.py:217
  2.8 19.8 %collective-permute-start.3 = (bf16[128,2048]{1,0:T(8,128)(2,1)}, bf16[128,2048]{1,0:T(8,128)(2,1)S(1)}, u32[]{:S(2)}, u32[]{:S(2)}) collective-permute-start(bf16[128,2048]{1,0:T(8,128)(2,1)} %param.16), channel_id=1, source_target_pairs={{12,3},{13,1},{14,19},{15,17},{28,0},{29,2},{30,16},{31,18}} | collective-permute-start | bytes 1572872 | tf_op jit(solution)/shard_map/ppermute | solution.py:217
  23.2 3.5 collective-permute-start.4
  23.9 2.8 collective-permute-start.5
  24.6 2.1 collective-permute-start.6
  25.3 1.4 collective-permute-start.7
  26.0 0.8 collective-permute-start.8
  26.8 3.5 collective-permute-start.10
  27.5 2.8 collective-permute-start.11
  28.2 2.1 collective-permute-start.12
  28.9 1.4 collective-permute-start.13
  29.6 0.8 collective-permute-start.9
  30.6 283.6 %copy-start.2 = (bf16[128,2048]{1,0:T(8,128)(2,1)}, bf16[128,2048]{1,0:T(8,128)(2,1)S(1)}, u32[]{:S(2)}) copy-start(bf16[128,2048]{1,0:T(8,128)(2,1)S(1)} %get-tuple-element.229) | copy-start | bytes 1572868
  30.6 265.9 %collective-permute-start.14 = (bf16[128,2048]{1,0:T(8,128)(2,1)S(1)}, bf16[128,2048]{1,0:T(8,128)(2,1)S(1)}, u32[]{:S(2)}, u32[]{:S(2)}) collective-permute-start(bf16[128,2048]{1,0:T(8,128)(2,1)S(1)} %get-tuple-element.229), channel_id=1, source_target_pairs={{8,12},{9,13},{10,14},{11,15},{24,28},{25,29},{26,30},{27,31}} | collective-permute-start | bytes 1572872 | tf_op jit(solution)/shard_map/ppermute | solution.py:234
  31.9 266.0 %collective-permute-start.15 = (bf16[128,2048]{1,0:T(8,128)(2,1)S(1)}, bf16[128,2048]{1,0:T(8,128)(2,1)S(1)}, u32[]{:S(2)}, u32[]{:S(2)}) collective-permute-start(bf16[128,2048]{1,0:T(8,128)(2,1)S(1)} %get-tuple-element.229), channel_id=1, source_target_pairs={{8,12},{9,14},{10,28},{11,30},{24,13},{25,15},{26,29},{27,31}} | collective-permute-start | bytes 1572872 | tf_op jit(solution)/shard_map/ppermute | solution.py:217
  33.2 276.5 %collective-permute-start.16 = (bf16[128,2048]{1,0:T(8,128)(2,1)S(1)}, bf16[128,2048]{1,0:T(8,128)(2,1)S(1)}, u32[]{:S(2)}, u32[]{:S(2)}) collective-permute-start(bf16[128,2048]{1,0:T(8,128)(2,1)S(1)} %get-tuple-element.229), channel_id=1, source_target_pairs={{8,13},{9,15},{10,29},{11,31},{24,14},{25,12},{26,30},{27,28}} | collective-permute-start | bytes 1572872 | tf_op jit(solution)/shard_map/ppermute | solution.py:217
  34.5 279.7 %collective-permute-start.17 = (bf16[128,2048]{1,0:T(8,128)(2,1)S(1)}, bf16[128,2048]{1,0:T(8,128)(2,1)S(1)}, u32[]{:S(2)}, u32[]{:S(2)}) collective-permute-start(bf16[128,2048]{1,0:T(8,128)(2,1)S(1)} %get-tuple-element.229), channel_id=1, source_target_pairs={{8,14},{9,12},{10,30},{11,28},{24,15},{25,13},{26,31},{27,29}} | collective-permute-start | bytes 1572872 | tf_op jit(solution)/shard_map/ppermute | solution.py:217
  35.8 278.4 %collective-permute-start.18 = (bf16[128,2048]{1,0:T(8,128)(2,1)S(1)}, bf16[128,2048]{1,0:T(8,128)(2,1)S(1)}, u32[]{:S(2)}, u32[]{:S(2)}) collective-permute-start(bf16[128,2048]{1,0:T(8,128)(2,1)S(1)} %get-tuple-element.229), channel_id=1, source_target_pairs={{8,15},{9,13},{10,31},{11,29},{24,12},{25,14},{26,28},{27,30}} | collective-permute-start | bytes 1572872 | tf_op jit(solution)/shard_map/ppermute | solution.py:217
  388.7 0.8 copy-start.1
